TPU v7x, 32 devices: a whole 2x2x4 slice. The times are simulated.
32 devices in a mesh: tm: 8 (over z, y), space: 4 (over x, core).
Axes of the slice: x: 2, y: 2, z: 4, core: 2. Of those that a mesh axis runs over, the one named last changes fastest.
Arguments:
- initial_state: float32 [32, 16, 128], P('space'), may hold values from -6 to 6
- initial_guess: float32 [8, 32, 16, 128], P('tm', 'space'), may hold values from -6 to 6
- region: int32 [32, 16, 128], P('space'), may hold values from 0 to 7
- conductivity: float32 [8], replicated, may hold values from 0.036 to 0.046
- loss_table: float32 [8], replicated, may hold values from 0.0003 to 0.06
- heat_gain: float32 [32, 16, 128], P('space'), may hold values from 0.5 to 2
- levels: float32 [8], replicated, may hold values from -1 to 3
- plan: int32 [96], P('tm'), may hold values from 0 to 7
Outputs:
- c_points: float32 [8, 32, 16, 128], P('tm', 'space')
- defect: float32 [8, 32, 16, 128], P('tm', 'space')
All inputs are finite; a program needn't handle non-finite values.
Results may differ from a plain program's by a relative error of at most 0.00009.
Values sent between devices are 32-bit elements; how exact they have to be, the bound alone decides.
A program may use at most 64 MiB of HBM per device.

v0:
```python
import jax
import jax.numpy as jnp
from jax import lax
from jax.sharding import PartitionSpec as P

M = 12
SWEEPS = 2


source_gain = 0.1
in_plane = 8.0


def extended(value, sides, width):
    for axis, dim in sides:
        devices, length = (lax.axis_size(axis), value.shape[dim])
        up = [(i, (i + 1) % devices) for i in range(devices - 1)]
        down = [(j, i) for i, j in up]
        last = lax.slice_in_dim(value, length - width, length, axis=dim)
        first = lax.slice_in_dim(value, 0, width, axis=dim)
        before = lax.ppermute(last, axis, up)
        after = lax.ppermute(first, axis, down)
        value = jnp.concatenate([before, value, after], axis=dim)
    return value


def shifted_2(block, axis, distance):
    devices = range(lax.axis_size(axis))
    route = [(i - distance, i) for i in devices if i - distance in devices]
    return lax.ppermute(block, axis, route)


def carried_in(value, axis, join, neutral):
    count, mine = (lax.axis_size(axis), lax.axis_index(axis))
    pieces = jax.tree.map(lambda part: lax.all_gather(part, axis), value)
    so_far = jax.tree.map(
        lambda part, zero: jnp.full_like(part, 0) + jnp.asarray(zero, part.dtype), value, neutral
    )

    def lap(position, so_far):
        longer = join(so_far, jax.tree.map(lambda part: part[position], pieces))
        return jax.tree.map(lambda new, old: jnp.where(position < mine, new, old), longer, so_far)

    return lax.fori_loop(0, count - 1, lap, so_far)


def lookup(index_array, table):
    total = jnp.zeros(index_array.shape, jnp.float32)
    for entry in range(table.shape[0]):
        total = jnp.where(index_array == entry, table[entry], total)
    return total


def advance(widened, spread, loss_rate, heat_gain, current):
    padded = jnp.pad(widened, ((0, 0), (1, 1), (1, 1)))
    centre = padded[1:-1, 1:-1, 1:-1]
    along = padded[2:, 1:-1, 1:-1] + padded[:-2, 1:-1, 1:-1]
    across = padded[1:-1, 2:, 1:-1] + padded[1:-1, :-2, 1:-1]
    across = across + padded[1:-1, 1:-1, 2:] + padded[1:-1, 1:-1, :-2]
    flow = in_plane * (along - 2.0 * centre) + (across - 4.0 * centre)
    return centre + spread * flow - loss_rate * centre + source_gain * current * heat_gain


def combine(earlier, latter):
    return (latter[0] * earlier[0], latter[0] * earlier[1] + latter[1])


def on_device(
    initial_state, initial_guess, region, conductivity, loss_table, heat_gain, levels, plan
):
    anchor = lax.axis_index("tm") == 0
    spread = lookup(region, conductivity)
    loss_rate = lookup(region, loss_table)
    coarse_factor = 1.0 / (1.0 + M * loss_rate)
    currents = lookup(plan, levels)

    def propagate(field_now):
        for step_index in range(M):
            widened = extended(field_now, (("space", 0),), 1)
            field_now = advance(widened, spread, loss_rate, heat_gain, currents[step_index])
        return field_now

    w_field = initial_guess[0]
    defect = jnp.zeros_like(initial_state)
    for sweep_index in range(SWEEPS):
        slice_end = propagate(w_field)
        received = shifted_2(slice_end, "tm", 1)
        slice_start = jnp.where(anchor, initial_state, received)
        relaxed = propagate(slice_start)
        defect = relaxed - slice_end
        identity = (jnp.ones_like(defect), jnp.zeros_like(defect))
        _, carried = carried_in((coarse_factor, defect), "tm", combine, identity)
        corrected = slice_end + (coarse_factor * carried + defect)
        shifted = shifted_2(corrected, "tm", 1)
        w_field = jnp.where(anchor, initial_state, shifted)
    return (w_field[None], defect[None])


def solution(mesh):
    placed = (
        P("space", None, None),
        P("tm", "space", None, None),
        P("space", None, None),
        P(),
        P(),
        P("space", None, None),
        P(),
        P("tm"),
    )
    return jax.shard_map(
        on_device,
        mesh=mesh,
        in_specs=placed,
        out_specs=(P("tm", "space", None, None), P("tm", "space", None, None)),
        check_vma=False,
    )
```

profile of v0, /device:TPU:30, one launch (start us, length us, event | category | flops | bytes accessed | tf_op | source)
XLA Modules:
  0.0 484.8 jit_solution(18207785123999704892)
XLA Ops:
  9.6 5.3 %compare_select_fusion.7 = f32[12]{0:T(128)S(1)} fusion(s32[12]{0:T(128)S(1)} %copy-done.6, f32[]{:T(128)} %bitcast.26, f32[]{:T(128)} %bitcast.25, f32[]{:T(128)} %bitcast.24, f32[]{:T(128)} %bitcast.23, f32[]{:T(128)} %bitcast.22, f32[]{:T(128)} %bitcast.21, f32[]{:T(128)} %bitcast.20, f32[]{:T(128)} %bitcast.19), kind=kLoop, calls=%fused_computation.809 | loop fusion | flops 192 | bytes 128 | tf_op jit(solution)/shard_map/jit(_where)/select_n | solution.py:50
  15.7 5.0 %add_divide_fusion = (f32[8,16,128]{2,1,0:T(8,128)S(1)}, f32[8,16,128]{2,1,0:T(8,128)S(1)}, pred[8,16,128]{2,1,0:T(8,128)(4,1)S(1)}, pred[8,16,128]{2,1,0:T(8,12...) fusion(f32[]{:T(128)} %bitcast.18, f32[]{:T(128)} %bitcast.17, ...), kind=kLoop, calls=%fused_computation.786 | loop fusion | flops 311296 | bytes 327712 | tf_op jit(solution)/shard_map/div | solution.py:74
  22.8 5.0 %fusion.435 = (f32[8,16,128]{2,1,0:T(8,128)S(1)}, f32[8,16,128]{2,1,0:T(8,128)S(1)}) fusion(f32[8,16,128]{2,1,0:T(8,128)S(1)} %bitcast.76, f32[10,18,130]{2,1,0:T(8,128)S(1)} %select_maximum_fusion.94, f32[1,16,128]{2,1,0:T(8,128)S(1)} %collective-permute-done.1, f32[1,16,128]{2,1,0:T(8,128)S(1)} %collective-permute-done, ...), kind=kLoop, calls=%fused_computation.775 | loop fusion | flops 425984 | bytes 737316 | tf_op jit(solution)/shard_map/add | solution.py:61
  27.8 3.2 collective-permute-start.2
  109.5 4.9 %collective-permute-done.24 = f32[8,16,128]{2,1,0:T(8,128)S(1)} collective-permute-done((f32[8,16,128]{2,1,0:T(8,128)S(1)}, f32[8,16,128]{2,1,0:T(8,128)S(1)}, u32[]{:S(2)}, u32[]{:S(2)}) %collective-permute-start.24) | collective-permute-done | bytes 65568 | tf_op jit(solution)/shard_map/ppermute | solution.py:30
  118.7 2.5 collective-permute-done.26
  125.9 2.5 collective-permute-done.28
  140.3 2.5 collective-permute-done.32
  147.4 2.5 collective-permute-done.34
  154.6 2.5 collective-permute-done.36
  169.0 2.5 collective-permute-done.40
  176.2 2.5 collective-permute-done.42
  197.7 31.4 %all-gather = f32[64,16,128]{2,1,0:T(8,128)S(1)} all-gather(f32[8,16,128]{2,1,0:T(8,128)S(1)} %get-tuple-element.248), channel_id=2, replica_groups=mesh['tm'=8,'space'=4] {'tm'}, dimensions={0}, use_global_device_ids=true | all-gather | bytes 589824 | tf_op jit(solution)/shard_map/all_gather | solution.py:35
  229.4 31.3 %all-gather.1 = f32[64,16,128]{2,1,0:T(8,128)S(1)} all-gather(f32[8,16,128]{2,1,0:T(8,128)S(1)} %fusion.228), channel_id=3, replica_groups=mesh['tm'=8,'space'=4] {'tm'}, dimensions={0}, use_global_device_ids=true | all-gather | bytes 589824 | tf_op jit(solution)/shard_map/all_gather | solution.py:35
  262.4 4.9 %collective-permute-done.49 = f32[8,16,128]{2,1,0:T(8,128)S(1)} collective-permute-done((f32[8,16,128]{2,1,0:T(8,128)S(1)}, f32[8,16,128]{2,1,0:T(8,128)S(1)}, u32[]{:S(2)}, u32[]{:S(2)}) %collective-permute-start.49) | collective-permute-done | bytes 65568 | tf_op jit(solution)/shard_map/ppermute | solution.py:30
  271.6 2.5 collective-permute-done.51
  278.8 2.5 collective-permute-done.53
  293.2 2.5 collective-permute-done.57
  300.4 2.5 collective-permute-done.59
  307.6 2.5 collective-permute-done.61
  329.3 2.5 collective-permute-done.67
  355.0 4.9 %collective-permute-done.74 = f32[8,16,128]{2,1,0:T(8,128)S(1)} collective-permute-done((f32[8,16,128]{2,1,0:T(8,128)S(1)}, f32[8,16,128]{2,1,0:T(8,128)S(1)}, u32[]{:S(2)}, u32[]{:S(2)}) %collective-permute-start.74) | collective-permute-done | bytes 65568 | tf_op jit(solution)/shard_map/ppermute | solution.py:30
  446.1 31.5 %all-gather.2 = f32[64,16,128]{2,1,0:T(8,128)S(1)} all-gather(f32[8,16,128]{2,1,0:T(8,128)S(1)} %fusion.11), channel_id=4, replica_groups=mesh['tm'=8,'space'=4] {'tm'}, dimensions={0}, use_global_device_ids=true | all-gather | bytes 589824 | tf_op jit(solution)/shard_map/all_gather | solution.py:35
  479.3 4.9 %collective-permute-done.99 = f32[8,16,128]{2,1,0:T(8,128)S(1)} collective-permute-done((f32[8,16,128]{2,1,0:T(8,128)S(1)}, f32[8,16,128]{2,1,0:T(8,128)S(1)}, u32[]{:S(2)}, u32[]{:S(2)}) %collective-permute-start.99) | collective-permute-done | bytes 65568 | tf_op jit(solution)/shard_map/ppermute | solution.py:30
  (367 shorter events, 309.0 us)
Async XLA Ops:
  1.4 20.6 %collective-permute-start = (f32[1,16,128]{2,1,0:T(8,128)S(1)}, f32[1,16,128]{2,1,0:T(8,128)S(1)}, u32[]{:S(2)}, u32[]{:S(2)}) collective-permute-start(f32[1,16,128]{2,1,0:T(8,128)S(1)} %get-tuple-element.355), channel_id=1, source_target_pairs={{1,0},{2,1},{3,2},{5,4},{6,5},{7,6},{9,8},{10,9},{11,10},{13,12},{... | collective-permute-start | bytes 24584 | tf_op jit(solution)/shard_map/ppermute | solution.py:22
  3.3 18.7 %collective-permute-start.1 = (f32[1,16,128]{2,1,0:T(8,128)S(1)}, f32[1,16,128]{2,1,0:T(8,128)S(1)}, u32[]{:S(2)}, u32[]{:S(2)}) collective-permute-start(f32[1,16,128]{2,1,0:T(8,128)S(1)} %get-tuple-element.354), channel_id=1, source_target_pairs={{0,1},{1,2},{2,3},{4,5},{5,6},{6,7},{8,9},{9,10},{10,11},{12,13},{... | collective-permute-start | bytes 24584 | tf_op jit(solution)/shard_map/ppermute | solution.py:21
  27.8 5.7 %collective-permute-start.2 = (f32[1,16,128]{2,1,0:T(8,128)S(1)}, f32[1,16,128]{2,1,0:T(8,128)S(1)}, u32[]{:S(2)}, u32[]{:S(2)}) collective-permute-start(f32[1,16,128]{2,1,0:T(8,128)S(1)} %get-tuple-element.353), channel_id=1, source_target_pairs={{1,0},{2,1},{3,2},{5,4},{6,5},{7,6},{9,8},{10,9},{11,10},{13,12},{... | collective-permute-start | bytes 24584 | tf_op jit(solution)/shard_map/ppermute | solution.py:22
  31.0 5.0 %collective-permute-start.3 = (f32[1,16,128]{2,1,0:T(8,128)S(1)}, f32[1,16,128]{2,1,0:T(8,128)S(1)}, u32[]{:S(2)}, u32[]{:S(2)}) collective-permute-start(f32[1,16,128]{2,1,0:T(8,128)S(1)} %get-tuple-element.352), channel_id=1, source_target_pairs={{0,1},{1,2},{2,3},{4,5},{5,6},{6,7},{8,9},{9,10},{10,11},{12,13},{... | collective-permute-start | bytes 24584 | tf_op jit(solution)/shard_map/ppermute | solution.py:21
  38.2 5.0 %collective-permute-start.5 = (f32[1,16,128]{2,1,0:T(8,128)S(1)}, f32[1,16,128]{2,1,0:T(8,128)S(1)}, u32[]{:S(2)}, u32[]{:S(2)}) collective-permute-start(f32[1,16,128]{2,1,0:T(8,128)S(1)} %get-tuple-element.350), channel_id=1, source_target_pairs={{0,1},{1,2},{2,3},{4,5},{5,6},{6,7},{8,9},{9,10},{10,11},{12,13},{... | collective-permute-start | bytes 24584 | tf_op jit(solution)/shard_map/ppermute | solution.py:21
  45.4 5.0 %collective-permute-start.7 = (f32[1,16,128]{2,1,0:T(8,128)S(1)}, f32[1,16,128]{2,1,0:T(8,128)S(1)}, u32[]{:S(2)}, u32[]{:S(2)}) collective-permute-start(f32[1,16,128]{2,1,0:T(8,128)S(1)} %get-tuple-element.348), channel_id=1, source_target_pairs={{0,1},{1,2},{2,3},{4,5},{5,6},{6,7},{8,9},{9,10},{10,11},{12,13},{... | collective-permute-start | bytes 24584 | tf_op jit(solution)/shard_map/ppermute | solution.py:21
  50.7 5.0 %collective-permute-start.8 = (f32[1,16,128]{2,1,0:T(8,128)S(1)}, f32[1,16,128]{2,1,0:T(8,128)S(1)}, u32[]{:S(2)}, u32[]{:S(2)}) collective-permute-start(f32[1,16,128]{2,1,0:T(8,128)S(1)} %get-tuple-element.347), channel_id=1, source_target_pairs={{1,0},{2,1},{3,2},{5,4},{6,5},{7,6},{9,8},{10,9},{11,10},{13,12},{... | collective-permute-start | bytes 24584 | tf_op jit(solution)/shard_map/ppermute | solution.py:22
  52.6 5.0 %collective-permute-start.9 = (f32[1,16,128]{2,1,0:T(8,128)S(1)}, f32[1,16,128]{2,1,0:T(8,128)S(1)}, u32[]{:S(2)}, u32[]{:S(2)}) collective-permute-start(f32[1,16,128]{2,1,0:T(8,128)S(1)} %get-tuple-element.346), channel_id=1, source_target_pairs={{0,1},{1,2},{2,3},{4,5},{5,6},{6,7},{8,9},{9,10},{10,11},{12,13},{... | collective-permute-start | bytes 24584 | tf_op jit(solution)/shard_map/ppermute | solution.py:21
  59.8 5.0 %collective-permute-start.11 = (f32[1,16,128]{2,1,0:T(8,128)S(1)}, f32[1,16,128]{2,1,0:T(8,128)S(1)}, u32[]{:S(2)}, u32[]{:S(2)}) collective-permute-start(f32[1,16,128]{2,1,0:T(8,128)S(1)} %get-tuple-element.344), channel_id=1, source_target_pairs={{0,1},{1,2},{2,3},{4,5},{5,6},{6,7},{8,9},{9,10},{10,11},{12,13},{... | collective-permute-start | bytes 24584 | tf_op jit(solution)/shard_map/ppermute | solution.py:21
  65.0 5.0 %collective-permute-start.12 = (f32[1,16,128]{2,1,0:T(8,128)S(1)}, f32[1,16,128]{2,1,0:T(8,128)S(1)}, u32[]{:S(2)}, u32[]{:S(2)}) collective-permute-start(f32[1,16,128]{2,1,0:T(8,128)S(1)} %get-tuple-element.343), channel_id=1, source_target_pairs={{1,0},{2,1},{3,2},{5,4},{6,5},{7,6},{9,8},{10,9},{11,10},{13,12},{... | collective-permute-start | bytes 24584 | tf_op jit(solution)/shard_map/ppermute | solution.py:22
  67.0 5.0 %collective-permute-start.13 = (f32[1,16,128]{2,1,0:T(8,128)S(1)}, f32[1,16,128]{2,1,0:T(8,128)S(1)}, u32[]{:S(2)}, u32[]{:S(2)}) collective-permute-start(f32[1,16,128]{2,1,0:T(8,128)S(1)} %get-tuple-element.342), channel_id=1, source_target_pairs={{0,1},{1,2},{2,3},{4,5},{5,6},{6,7},{8,9},{9,10},{10,11},{12,13},{... | collective-permute-start | bytes 24584 | tf_op jit(solution)/shard_map/ppermute | solution.py:21
  72.2 5.0 %collective-permute-start.14 = (f32[1,16,128]{2,1,0:T(8,128)S(1)}, f32[1,16,128]{2,1,0:T(8,128)S(1)}, u32[]{:S(2)}, u32[]{:S(2)}) collective-permute-start(f32[1,16,128]{2,1,0:T(8,128)S(1)} %get-tuple-element.341), channel_id=1, source_target_pairs={{1,0},{2,1},{3,2},{5,4},{6,5},{7,6},{9,8},{10,9},{11,10},{13,12},{... | collective-permute-start | bytes 24584 | tf_op jit(solution)/shard_map/ppermute | solution.py:22
  74.1 5.0 %collective-permute-start.15 = (f32[1,16,128]{2,1,0:T(8,128)S(1)}, f32[1,16,128]{2,1,0:T(8,128)S(1)}, u32[]{:S(2)}, u32[]{:S(2)}) collective-permute-start(f32[1,16,128]{2,1,0:T(8,128)S(1)} %get-tuple-element.340), channel_id=1, source_target_pairs={{0,1},{1,2},{2,3},{4,5},{5,6},{6,7},{8,9},{9,10},{10,11},{12,13},{... | collective-permute-start | bytes 24584 | tf_op jit(solution)/shard_map/ppermute | solution.py:21
  79.4 5.0 %collective-permute-start.16 = (f32[1,16,128]{2,1,0:T(8,128)S(1)}, f32[1,16,128]{2,1,0:T(8,128)S(1)}, u32[]{:S(2)}, u32[]{:S(2)}) collective-permute-start(f32[1,16,128]{2,1,0:T(8,128)S(1)} %get-tuple-element.339), channel_id=1, source_target_pairs={{1,0},{2,1},{3,2},{5,4},{6,5},{7,6},{9,8},{10,9},{11,10},{13,12},{... | collective-permute-start | bytes 24584 | tf_op jit(solution)/shard_map/ppermute | solution.py:22
  81.3 5.0 %collective-permute-start.17 = (f32[1,16,128]{2,1,0:T(8,128)S(1)}, f32[1,16,128]{2,1,0:T(8,128)S(1)}, u32[]{:S(2)}, u32[]{:S(2)}) collective-permute-start(f32[1,16,128]{2,1,0:T(8,128)S(1)} %get-tuple-element.338), channel_id=1, source_target_pairs={{0,1},{1,2},{2,3},{4,5},{5,6},{6,7},{8,9},{9,10},{10,11},{12,13},{... | collective-permute-start | bytes 24584 | tf_op jit(solution)/shard_map/ppermute | solution.py:21
  86.6 5.0 %collective-permute-start.18 = (f32[1,16,128]{2,1,0:T(8,128)S(1)}, f32[1,16,128]{2,1,0:T(8,128)S(1)}, u32[]{:S(2)}, u32[]{:S(2)}) collective-permute-start(f32[1,16,128]{2,1,0:T(8,128)S(1)} %get-tuple-element.337), channel_id=1, source_target_pairs={{1,0},{2,1},{3,2},{5,4},{6,5},{7,6},{9,8},{10,9},{11,10},{13,12},{... | collective-permute-start | bytes 24584 | tf_op jit(solution)/shard_map/ppermute | solution.py:22
  93.8 5.0 %collective-permute-start.20 = (f32[1,16,128]{2,1,0:T(8,128)S(1)}, f32[1,16,128]{2,1,0:T(8,128)S(1)}, u32[]{:S(2)}, u32[]{:S(2)}) collective-permute-start(f32[1,16,128]{2,1,0:T(8,128)S(1)} %get-tuple-element.335), channel_id=1, source_target_pairs={{1,0},{2,1},{3,2},{5,4},{6,5},{7,6},{9,8},{10,9},{11,10},{13,12},{... | collective-permute-start | bytes 24584 | tf_op jit(solution)/shard_map/ppermute | solution.py:22
  101.0 5.0 %collective-permute-start.22 = (f32[1,16,128]{2,1,0:T(8,128)S(1)}, f32[1,16,128]{2,1,0:T(8,128)S(1)}, u32[]{:S(2)}, u32[]{:S(2)}) collective-permute-start(f32[1,16,128]{2,1,0:T(8,128)S(1)} %get-tuple-element.333), channel_id=1, source_target_pairs={{1,0},{2,1},{3,2},{5,4},{6,5},{7,6},{9,8},{10,9},{11,10},{13,12},{... | collective-permute-start | bytes 24584 | tf_op jit(solution)/shard_map/ppermute | solution.py:22
  108.2 6.2 %collective-permute-start.24 = (f32[8,16,128]{2,1,0:T(8,128)S(1)}, f32[8,16,128]{2,1,0:T(8,128)S(1)}, u32[]{:S(2)}, u32[]{:S(2)}) collective-permute-start(f32[8,16,128]{2,1,0:T(8,128)S(1)} %fusion.336), channel_id=1, source_target_pairs={{0,4},{4,8},{8,12},{12,16},{16,20},{20,24},{24,28},{1,5},{5,9},{9,... | collective-permute-start | bytes 196616 | tf_op jit(solution)/shard_map/ppermute | solution.py:30
  193.4 35.7 %collective-permute-start.47 = (f32[1,16,128]{2,1,0:T(8,128)S(1)}, f32[1,16,128]{2,1,0:T(8,128)S(1)}, u32[]{:S(2)}, u32[]{:S(2)}) collective-permute-start(f32[1,16,128]{2,1,0:T(8,128)S(1)} %get-tuple-element.309), channel_id=1, source_target_pairs={{1,0},{2,1},{3,2},{5,4},{6,5},{7,6},{9,8},{10,9},{11,10},{13,12},{... | collective-permute-start | bytes 24584 | tf_op jit(solution)/shard_map/ppermute | solution.py:22
  195.3 33.8 %collective-permute-start.48 = (f32[1,16,128]{2,1,0:T(8,128)S(1)}, f32[1,16,128]{2,1,0:T(8,128)S(1)}, u32[]{:S(2)}, u32[]{:S(2)}) collective-permute-start(f32[1,16,128]{2,1,0:T(8,128)S(1)} %get-tuple-element.308), channel_id=1, source_target_pairs={{0,1},{1,2},{2,3},{4,5},{5,6},{6,7},{8,9},{9,10},{10,11},{12,13},{... | collective-permute-start | bytes 24584 | tf_op jit(solution)/shard_map/ppermute | solution.py:21
  261.1 6.2 %collective-permute-start.49 = (f32[8,16,128]{2,1,0:T(8,128)S(1)}, f32[8,16,128]{2,1,0:T(8,128)S(1)}, u32[]{:S(2)}, u32[]{:S(2)}) collective-permute-start(f32[8,16,128]{2,1,0:T(8,128)S(1)} %add_add_fusion.1), channel_id=1, source_target_pairs={{0,4},{4,8},{8,12},{12,16},{16,20},{20,24},{24,28},{1,5},{5,9},{9,... | collective-permute-start | bytes 196616 | tf_op jit(solution)/shard_map/ppermute | solution.py:30
  353.7 6.2 %collective-permute-start.74 = (f32[8,16,128]{2,1,0:T(8,128)S(1)}, f32[8,16,128]{2,1,0:T(8,128)S(1)}, u32[]{:S(2)}, u32[]{:S(2)}) collective-permute-start(f32[8,16,128]{2,1,0:T(8,128)S(1)} %fusion.119), channel_id=1, source_target_pairs={{0,4},{4,8},{8,12},{12,16},{16,20},{20,24},{24,28},{1,5},{5,9},{9,... | collective-permute-start | bytes 196616 | tf_op jit(solution)/shard_map/ppermute | solution.py:30
  478.0 6.2 %collective-permute-start.99 = (f32[8,16,128]{2,1,0:T(8,128)S(1)}, f32[8,16,128]{2,1,0:T(8,128)S(1)}, u32[]{:S(2)}, u32[]{:S(2)}) collective-permute-start(f32[8,16,128]{2,1,0:T(8,128)S(1)} %add_add_fusion), channel_id=1, source_target_pairs={{0,4},{4,8},{8,12},{12,16},{16,20},{20,24},{24,28},{1,5},{5,9},{9,... | collective-permute-start | bytes 196616 | tf_op jit(solution)/shard_map/ppermute | solution.py:30
  (83 other events, 421.8 us)
where the time goes:
time: 488 us; the launch traced here: 485 us
  starting transfers between devices  214 us (44%)
  waiting for transfers between devices  130 us (27%)
  blocking collectives  94.2 us (19%)
  other arithmetic  28.8 us (6%)
  between operations  10.7 us (2%)
  local copies, waits for them, and re-layouts  6.92 us (1%)
    ppermute x48, starting transfers between devices, extended(): before = lax.ppermute(last, axis, up)  115 us
    ppermute x48, waiting for transfers between devices, extended(): before = lax.ppermute(last, axis, up)  111 us
    all_gather x3, blocking collectives, carried_in(): pieces = jax.tree.map(lambda part: lax.all_gather(part, axis), value)  94.2 us
    ppermute x48, starting transfers between devices, extended(): after = lax.ppermute(first, axis, down)  93.6 us
    ppermute x4, waiting for transfers between devices, shifted_2(): return lax.ppermute(block, axis, route)  19.4 us
    add x46, other arithmetic, advance(): centre + spread * flow - loss_rate * centre  10.9 us
  transfers between devices with their start and end apart: 100, of which 50 were waited for; matrix products, arithmetic and copies ran while one was open for 3% of the time, Pallas kernels for 0%

commit v1 on v0

v1 whole, which is shorter than its diff:
```python
import functools

import jax
import jax.numpy as jnp
from jax import lax
from jax.experimental import pallas as pl
from jax.experimental.pallas import tpu as pltpu
from jax.sharding import PartitionSpec as P

M = 12
MESH = pl.DeviceIdType.MESH

GROUP = 4


def halo_pieces(block):
    pieces, left, distance = [], M, 1
    while left > 0:
        pieces.append((distance, min(block, left)))
        left -= block
        distance += 1
    return pieces


def scan_distances(count):
    distances = []
    while not distances or distances[-1] * 2 < count:
        distances.append(distances[-1] * 2 if distances else 1)
    return [d for d in distances if d < count]


def kernel(
    times, spaces, block,
    w_ref, region_ref, gain_ref, init_ref, conduct_ref, loss_ref, levels_ref, plan_ref,
    out_ref, defect_ref,
    shift_src, shift_dst, region_buf, gain_buf, fields, other, diag_buf, spread_buf, factor_buf,
    sends, scan_src, scan_dst, kept,
    halo_send, halo_recv, shift_sems, scan_send, scan_recv,
):
    k, s = lax.axis_index("tm"), lax.axis_index("space")
    pieces = halo_pieces(block)
    distances = scan_distances(times)
    whole = block + 2 * M
    own = pl.ds(M, block)
    ny, nz = region_ref.shape[1:]

    barrier = pltpu.get_barrier_semaphore()
    expected = jnp.int32(0)
    for axis, mine, count, steps in (
        ("space", s, spaces, [d for d, _ in pieces]),
        ("tm", k, times, distances),
    ):
        for d in steps:
            for peer in (mine - d, mine + d):
                there = jnp.logical_and(peer >= 0, peer < count)
                expected = expected + there.astype(jnp.int32)

                @pl.when(there)
                def _(axis=axis, peer=peer):
                    pl.semaphore_signal(barrier, inc=1, device_id={axis: peer}, device_id_type=MESH)

    pl.semaphore_wait(barrier, expected)

    def halo_copies(number, source, target):
        out, into = [], []
        for at, (d, planes) in enumerate(pieces):
            low = M - (d - 1) * block - planes
            high = M + d * block
            for side, (first, place) in enumerate(((block - planes, low), (0, high))):
                to = s + d if side == 0 else s - d
                origin = s - d if side == 0 else s + d
                copy = pltpu.make_async_remote_copy(
                    src_ref=source.at[pl.ds(first, planes)],
                    dst_ref=target.at[pl.ds(place, planes)],
                    send_sem=halo_send.at[number, 2 * at + side],
                    recv_sem=halo_recv.at[number, 2 * at + side],
                    device_id={"space": to},
                    device_id_type=MESH,
                )
                out.append((jnp.logical_and(to >= 0, to < spaces), copy))
                into.append((jnp.logical_and(origin >= 0, origin < spaces), copy))
        return out, into

    def start(copies):
        for there, copy in copies:
            pl.when(there)(copy.start)

    def finish(copies):
        for there, copy in copies:
            pl.when(there)(copy.wait_recv)

    def drain(copies):
        for there, copy in copies:
            pl.when(there)(copy.wait_send)

    shift_src[pl.ds(0, block)] = w_ref[0]
    rows = lax.broadcasted_iota(jnp.int32, (ny, nz), 0)
    currents = jnp.zeros((ny, nz), jnp.float32)
    for step in range(M):
        currents = jnp.where(rows == step, 0.1 * levels_ref[plan_ref[step]], currents)
    shift_src[block] = currents
    has_before, has_after = k > 0, k < times - 1
    shift = pltpu.make_async_remote_copy(
        src_ref=shift_src, dst_ref=shift_dst, send_sem=shift_sems.at[0], recv_sem=shift_sems.at[1],
        device_id={"tm": k + 1}, device_id_type=MESH,
    )
    pl.when(has_after)(shift.start)

    region_out, region_in = halo_copies(0, region_ref, region_buf)
    gain_out, gain_in = halo_copies(1, gain_ref, gain_buf)
    start(region_out)
    start(gain_out)

    for d, planes in pieces:
        low = M - (d - 1) * block - planes
        high = M + d * block

        for there, place in ((s - d < 0, low), (s + d >= spaces, high)):
            @pl.when(there)
            def _(place=place, planes=planes):
                zero = jnp.zeros((planes, ny, nz), jnp.float32)
                region_buf[pl.ds(place, planes)] = jnp.full((planes, ny, nz), -1, jnp.int32)
                gain_buf[pl.ds(place, planes)] = zero
                for number in range(4):
                    fields[number, pl.ds(place, planes)] = zero

    region_buf[own] = region_ref[...]
    gain_buf[own] = gain_ref[...]

    @pl.when(k == 0)
    def _():
        shift_dst[...] = jnp.zeros_like(shift_dst)

    for at, d in enumerate(distances):
        @pl.when(k < d)
        def _(at=at):
            for scan in range(2):
                scan_dst[scan, at] = jnp.zeros((block, ny, nz), jnp.float32)

    pl.when(has_before)(shift.wait_recv)
    w_out, w_in = halo_copies(2, shift_dst, fields.at[0])
    start(w_out)
    fields[0, own] = shift_dst[pl.ds(0, block)]

    finish(region_in)

    def coefficients(p, _):
        index = region_buf[p]
        spread = jnp.zeros((ny, nz), jnp.float32)
        loss = jnp.zeros((ny, nz), jnp.float32)
        for entry in range(conduct_ref.shape[0]):
            here = index == entry
            spread = jnp.where(here, conduct_ref[entry], spread)
            loss = jnp.where(here, loss_ref[entry], loss)
        inside = jnp.where(index >= 0, 1.0, 0.0)
        spread_buf[p] = spread
        diag_buf[p] = inside - 20.0 * spread - loss
        factor_buf[p] = 1.0 / (1.0 + M * loss)
        return 0

    lax.fori_loop(0, whole, coefficients, 0)
    finish(gain_in)
    finish(w_in)

    lane = lax.broadcasted_iota(jnp.int32, (ny, nz), 1)
    first_lane, last_lane = lane == 0, lane == nz - 1
    first_row, last_row = rows == 0, rows == ny - 1

    def fine_step(source, target, margin, current):
        def plane(p, _):
            v = source[p]
            along = source[p - 1] + source[p + 1]
            across = jnp.where(first_lane, 0.0, pltpu.roll(v, 1, 1))
            across += jnp.where(last_lane, 0.0, pltpu.roll(v, nz - 1, 1))
            across += jnp.where(first_row, 0.0, pltpu.roll(v, 1, 0))
            across += jnp.where(last_row, 0.0, pltpu.roll(v, ny - 1, 0))
            new = diag_buf[p] * v + spread_buf[p] * (8.0 * along + across)
            if current is not None:
                new = new + current * gain_buf[p]
            target[p] = new
            return 0

        lax.fori_loop(margin, whole - margin, plane, 0, unroll=True)

    def propagate(field, sourced):
        for group in range(M // GROUP):
            margin = group * GROUP + 1

            def pair(at, _, group=group, margin=margin):
                step = group * GROUP + 2 * at
                for half, (source, target) in enumerate(((field, other), (other, field))):
                    current = None
                    if sourced:
                        row = shift_dst[block, pl.ds(step + half, 1), :]
                        current = jnp.broadcast_to(row, (ny, nz))
                    fine_step(source, target, margin, current)
                return 0

            lax.fori_loop(0, GROUP // 2, pair, 0)

    def exchange(number, value):
        sends[number - 3] = value
        out, into = halo_copies(number, sends.at[number - 3], fields.at[number - 2])
        start(out)
        fields[number - 2, own] = value
        finish(into)
        return out

    pending = []

    def scan(number, value, factor):
        power = factor
        for at, d in enumerate(distances):
            scan_src[number, at] = value
            copy = pltpu.make_async_remote_copy(
                src_ref=scan_src.at[number, at], dst_ref=scan_dst.at[number, at],
                send_sem=scan_send.at[number, at], recv_sem=scan_recv.at[number, at],
                device_id={"tm": k + d}, device_id_type=MESH,
            )
            pl.when(k + d < times)(copy.start)
            pl.when(k >= d)(copy.wait_recv)
            pending.append((k + d < times, copy))
            if at + 1 < len(distances):
                value = value + power * scan_dst[number, at]
                power = power * power

    def two_back(number, factor):
        square = factor * factor
        powers = [square]
        for _ in distances[2:]:
            powers.append(powers[-1] * powers[-1])
        total = jnp.zeros((block, ny, nz), jnp.float32)
        for at in reversed(range(1, len(distances))):
            total = scan_dst[number, at] + (powers[at - 1] * total if at + 1 < len(distances) else 0.0)
        return total

    propagate(fields.at[0], True)
    before = jnp.where(k == 0, init_ref[...], fields[0, own])
    kept[0] = before
    out_1 = exchange(3, before - w_ref[0])
    propagate(fields.at[1], False)

    factor = factor_buf[own]
    scan(0, fields[1, own], factor)
    carried = two_back(0, factor)
    out_2 = exchange(4, carried)
    propagate(fields.at[2], False)

    relaxed = fields[2, own]
    kept[0] = kept[0] + scan_dst[0, 0] + relaxed
    out_3 = exchange(5, relaxed - factor * sends[1])
    propagate(fields.at[3], False)
    defect = fields[3, own]
    defect_ref[0] = defect

    scan(1, defect, factor)
    corrected = kept[0] + scan_dst[1, 0] + factor * two_back(1, factor)
    out_ref[0] = jnp.where(k == 0, init_ref[...], corrected)

    pl.when(has_after)(shift.wait_send)
    for copies in (region_out, gain_out, w_out, out_1, out_2, out_3, pending):
        drain(copies)


def on_device(
    times, spaces,
    initial_state, initial_guess, region, conductivity, loss_table, heat_gain, levels, plan,
):
    block, ny, nz = region.shape
    whole = block + 2 * M
    pieces, laps = 2 * len(halo_pieces(block)), len(scan_distances(times))
    vmem = pl.BlockSpec(memory_space=pltpu.VMEM)
    smem = pl.BlockSpec(memory_space=pltpu.SMEM)
    f32 = jnp.float32
    return pl.pallas_call(
        functools.partial(kernel, times, spaces, block),
        out_shape=(jax.ShapeDtypeStruct((1, block, ny, nz), f32),) * 2,
        in_specs=[vmem] * 4 + [smem] * 4,
        out_specs=(vmem, vmem),
        scratch_shapes=[
            pltpu.VMEM((block + 1, ny, nz), f32),
            pltpu.VMEM((block + 1, ny, nz), f32),
            pltpu.VMEM((whole, ny, nz), jnp.int32),
            pltpu.VMEM((whole, ny, nz), f32),
            pltpu.VMEM((4, whole, ny, nz), f32),
            pltpu.VMEM((whole, ny, nz), f32),
            pltpu.VMEM((whole, ny, nz), f32),
            pltpu.VMEM((whole, ny, nz), f32),
            pltpu.VMEM((whole, ny, nz), f32),
            pltpu.VMEM((3, block, ny, nz), f32),
            pltpu.VMEM((2, laps, block, ny, nz), f32),
            pltpu.VMEM((2, laps, block, ny, nz), f32),
            pltpu.VMEM((1, block, ny, nz), f32),
            pltpu.SemaphoreType.DMA((6, pieces)),
            pltpu.SemaphoreType.DMA((6, pieces)),
            pltpu.SemaphoreType.DMA((2,)),
            pltpu.SemaphoreType.DMA((2, laps)),
            pltpu.SemaphoreType.DMA((2, laps)),
        ],
        compiler_params=pltpu.CompilerParams(
            collective_id=0, has_side_effects=True, vmem_limit_bytes=16 * 1024 * 1024
        ),
    )(initial_guess, region, heat_gain, initial_state, conductivity, loss_table, levels, plan)


def solution(mesh):
    placed = (
        P("space", None, None),
        P("tm", "space", None, None),
        P("space", None, None),
        P(),
        P(),
        P("space", None, None),
        P(),
        P("tm"),
    )
    return jax.shard_map(
        functools.partial(on_device, mesh.shape["tm"], mesh.shape["space"]),
        mesh=mesh,
        in_specs=placed,
        out_specs=(P("tm", "space", None, None), P("tm", "space", None, None)),
        check_vma=False,
    )
```

time: 488 us -> 47 us (0.10)
  starting transfers between devices: 214 us -> 0 us
  waiting for transfers between devices: 130 us -> 0 us
  blocking collectives: 94.2 us -> 0 us
  Pallas kernels: 0 us -> 38.8 us
  other arithmetic: 28.8 us -> 0 us
  between operations: 10.7 us -> 0.66 us
    ppermute x100 -> x0, starting transfers between devices: 214 us -> none  [the longest x48 115 us: extended(): before = lax.ppermute(last, axis, up)]
    ppermute x100 -> x0, waiting for transfers between devices: 130 us -> none  [the longest x48 111 us: extended(): before = lax.ppermute(last, axis, up)]
    all_gather x3 -> x0, blocking collectives: 94.2 us -> none  [carried_in(): pieces = jax.tree.map(lambda part: lax.all_gather(part, axis), value)]
    pallas_call x0 -> x1, Pallas kernels: none -> 38.8 us  [on_device(): pl.pallas_call(functools.partial(kernel, times, spaces, block), out_shape...]
    add x48 -> x0, other arithmetic: 11 us -> none  [the longest x46 10.9 us: advance(): centre + spread * flow - loss_rate * centre]
    concatenate x48 -> x0, other arithmetic: 6.29 us -> none  [extended(): value = jnp.concatenate([before, value, after], axis=dim)]
    unnamed x14 -> x18, local copies, waits for them, and re-layouts: 1.38 us -> 7.23 us
    select_n x18 -> x0, other arithmetic: 5.56 us -> none  [the longest x1 5.3 us: lookup(): total = jnp.where(index_array == entry, table[entry], total)]
  transfers between devices with their start and end apart: 100 -> 0, of which waited for: 50 -> 0; matrix products, arithmetic and copies ran while one was open for 3% -> 0% of each run, Pallas kernels for 0% -> 0%
where the time goes in v1:
time: 47 us; the launch traced here: 46.6 us
  Pallas kernels  38.8 us (83%)
  local copies, waits for them, and re-layouts  7.23 us (15%)
  between operations  0.66 us (1%)
    pallas_call x1, Pallas kernels, on_device(): pl.pallas_call(functools.partial(kernel, times, spaces, block), out_shape...  38.8 us
    unnamed x18, local copies, waits for them, and re-layouts  7.23 us

profile of v1, /device:TPU:30, one launch (start us, length us, event | category | flops | bytes accessed | tf_op | source)
XLA Modules:
  0.0 46.6 jit_solution(12343846016713935894)
XLA Ops:
  0.6 0.0 copy-start
  0.6 0.8 %copy-done = f32[1,8,16,128]{3,2,1,0:T(8,128)S(1)} copy-done((f32[1,8,16,128]{3,2,1,0:T(8,128)S(1)}, f32[1,8,16,128]{3,2,1,0:T(8,128)}, u32[]{:S(2)}) %copy-start) | copy-done | bytes 65560
  1.5 0.0 copy-start.1
  1.5 0.8 %copy-done.1 = s32[8,16,128]{2,1,0:T(8,128)S(1)} copy-done((s32[8,16,128]{2,1,0:T(8,128)S(1)}, s32[8,16,128]{2,1,0:T(8,128)}, u32[]{:S(2)}) %copy-start.1) | copy-done | bytes 65560
  2.3 0.0 copy-start.2
  2.3 0.8 %copy-done.2 = f32[8,16,128]{2,1,0:T(8,128)S(1)} copy-done((f32[8,16,128]{2,1,0:T(8,128)S(1)}, f32[8,16,128]{2,1,0:T(8,128)}, u32[]{:S(2)}) %copy-start.2) | copy-done | bytes 65560
  3.2 0.0 copy-start.3
  3.2 0.8 %copy-done.3 = f32[8,16,128]{2,1,0:T(8,128)S(1)} copy-done((f32[8,16,128]{2,1,0:T(8,128)S(1)}, f32[8,16,128]{2,1,0:T(8,128)}, u32[]{:S(2)}) %copy-start.3) | copy-done | bytes 65560
  4.0 0.0 copy-start.4
  4.0 0.7 %copy-done.4 = f32[8]{0:T(128)S(1)} copy-done((f32[8]{0:T(128)S(1)}, f32[8]{0:T(128)}, u32[]{:S(2)}) %copy-start.4) | copy-done | bytes 56
  4.6 0.0 copy-start.5
  4.7 0.7 %copy-done.5 = f32[8]{0:T(128)S(1)} copy-done((f32[8]{0:T(128)S(1)}, f32[8]{0:T(128)}, u32[]{:S(2)}) %copy-start.5) | copy-done | bytes 56
  5.3 0.0 copy-start.6
  5.3 0.7 %copy-done.6 = f32[8]{0:T(128)S(1)} copy-done((f32[8]{0:T(128)S(1)}, f32[8]{0:T(128)}, u32[]{:S(2)}) %copy-start.6) | copy-done | bytes 56
  6.0 0.0 copy-start.7
  6.0 0.7 %copy-done.7 = s32[12]{0:T(128)S(1)} copy-done((s32[12]{0:T(128)S(1)}, s32[12]{0:T(128)}, u32[]{:S(2)}) %copy-start.7) | copy-done | bytes 72
  6.6 38.8 %shard_map.95 = (f32[1,8,16,128]{3,2,1,0:T(8,128)S(1)}, f32[1,8,16,128]{3,2,1,0:T(8,128)S(1)}) custom-call(f32[1,8,16,128]{3,2,1,0:T(8,128)S(1)} %copy-done, s32[8,16,128]{2,1,0:T(8,128)S(1)} %copy-done.1, f32[8,16,128]{2,1,0:T(8,128)S(1)} %copy-done.2, f32[8,16,128]{2,1,0:T(8,128)S(1)} %copy-done.3, f32[8]{0:T(128)S(1)} %copy-done.4, f32[8]{0:T(128)S(1)} %copy-done.5, ...), custom_call_target="tpu_custom_call" | custom-call | tf_op jit(solution)/shard_map/pallas_call | solution.py:275
  45.4 0.6 %copy.12 = f32[1,8,16,128]{3,2,1,0:T(8,128)} copy(f32[1,8,16,128]{3,2,1,0:T(8,128)S(1)} %get-tuple-element.4) | data formatting | bytes 131072
  46.0 0.6 %copy.13 = f32[1,8,16,128]{3,2,1,0:T(8,128)} copy(f32[1,8,16,128]{3,2,1,0:T(8,128)S(1)} %get-tuple-element.5) | data formatting | bytes 131072
Async XLA Ops:
  0.6 0.8 %copy-start = (f32[1,8,16,128]{3,2,1,0:T(8,128)S(1)}, f32[1,8,16,128]{3,2,1,0:T(8,128)}, u32[]{:S(2)}) copy-start(f32[1,8,16,128]{3,2,1,0:T(8,128)} %w_ref.1) | copy-start | bytes 196612
  1.5 0.8 %copy-start.1 = (s32[8,16,128]{2,1,0:T(8,128)S(1)}, s32[8,16,128]{2,1,0:T(8,128)}, u32[]{:S(2)}) copy-start(s32[8,16,128]{2,1,0:T(8,128)} %region_ref.1) | copy-start | bytes 196612
  2.3 0.8 %copy-start.2 = (f32[8,16,128]{2,1,0:T(8,128)S(1)}, f32[8,16,128]{2,1,0:T(8,128)}, u32[]{:S(2)}) copy-start(f32[8,16,128]{2,1,0:T(8,128)} %gain_ref.1) | copy-start | bytes 196612
  3.2 0.8 %copy-start.3 = (f32[8,16,128]{2,1,0:T(8,128)S(1)}, f32[8,16,128]{2,1,0:T(8,128)}, u32[]{:S(2)}) copy-start(f32[8,16,128]{2,1,0:T(8,128)} %init_ref.1) | copy-start | bytes 196612
  4.0 0.7 %copy-start.4 = (f32[8]{0:T(128)S(1)}, f32[8]{0:T(128)}, u32[]{:S(2)}) copy-start(f32[8]{0:T(128)} %conduct_ref.1) | copy-start | bytes 100
  4.6 0.7 %copy-start.5 = (f32[8]{0:T(128)S(1)}, f32[8]{0:T(128)}, u32[]{:S(2)}) copy-start(f32[8]{0:T(128)} %loss_ref.1) | copy-start | bytes 100
  5.3 0.7 %copy-start.6 = (f32[8]{0:T(128)S(1)}, f32[8]{0:T(128)}, u32[]{:S(2)}) copy-start(f32[8]{0:T(128)} %levels_ref.1) | copy-start | bytes 100
  6.0 0.7 %copy-start.7 = (s32[12]{0:T(128)S(1)}, s32[12]{0:T(128)}, u32[]{:S(2)}) copy-start(s32[12]{0:T(128)} %plan_ref.1) | copy-start | bytes 148

commit v2 on v1

--- a/solution.py
+++ b/solution.py
@@ -10,7 +10,7 @@
 M = 12
 MESH = pl.DeviceIdType.MESH
 
-GROUP = 4
+GROUP = 2
 
 
 def halo_pieces(block):
@@ -31,11 +31,12 @@
 
 def kernel(
     times, spaces, block,
-    w_ref, region_ref, gain_ref, init_ref, conduct_ref, loss_ref, levels_ref, plan_ref,
+    w_ref, region_ref, gain_ref, init_ref, conduct_hbm, loss_hbm, levels_hbm, plan_hbm,
     out_ref, defect_ref,
-    shift_src, shift_dst, region_buf, gain_buf, fields, other, diag_buf, spread_buf, factor_buf,
+    w_buf, init_buf, conduct_ref, loss_ref, levels_ref, plan_ref,
+    current_src, current_dst, shift_dst, region_buf, gain_buf, fields, other, diag_buf, spread_buf, factor_buf,
     sends, scan_src, scan_dst, kept,
-    halo_send, halo_recv, shift_sems, scan_send, scan_recv,
+    halo_send, halo_recv, shift_sems, scan_send, scan_recv, load_sems,
 ):
     k, s = lax.axis_index("tm"), lax.axis_index("space")
     pieces = halo_pieces(block)
@@ -43,6 +44,17 @@
     whole = block + 2 * M
     own = pl.ds(M, block)
     ny, nz = region_ref.shape[1:]
+
+    loads = [
+        pltpu.make_async_copy(source, target, load_sems.at[at])
+        for at, (source, target) in enumerate((
+            (levels_hbm, levels_ref), (plan_hbm, plan_ref), (conduct_hbm, conduct_ref),
+            (loss_hbm, loss_ref), (region_ref, region_buf.at[own]), (gain_ref, gain_buf.at[own]),
+            (w_ref.at[0], w_buf), (init_ref, init_buf),
+        ))
+    ]
+    for load in loads:
+        load.start()
 
     barrier = pltpu.get_barrier_semaphore()
     expected = jnp.int32(0)
@@ -93,23 +105,30 @@
         for there, copy in copies:
             pl.when(there)(copy.wait_send)
 
-    shift_src[pl.ds(0, block)] = w_ref[0]
+    has_before, has_after = k > 0, k < times - 1
+    shift = pltpu.make_async_remote_copy(
+        src_ref=w_ref.at[0], dst_ref=shift_dst, send_sem=shift_sems.at[0], recv_sem=shift_sems.at[1],
+        device_id={"tm": k + 1}, device_id_type=MESH,
+    )
+    pl.when(has_after)(shift.start)
+
+    region_out, region_in = halo_copies(0, region_ref, region_buf)
+    gain_out, gain_in = halo_copies(1, gain_ref, gain_buf)
+    start(region_out)
+    start(gain_out)
+
+    for load in loads[:2]:
+        load.wait()
     rows = lax.broadcasted_iota(jnp.int32, (ny, nz), 0)
     currents = jnp.zeros((ny, nz), jnp.float32)
     for step in range(M):
         currents = jnp.where(rows == step, 0.1 * levels_ref[plan_ref[step]], currents)
-    shift_src[block] = currents
-    has_before, has_after = k > 0, k < times - 1
-    shift = pltpu.make_async_remote_copy(
-        src_ref=shift_src, dst_ref=shift_dst, send_sem=shift_sems.at[0], recv_sem=shift_sems.at[1],
+    current_src[...] = currents
+    current_shift = pltpu.make_async_remote_copy(
+        src_ref=current_src, dst_ref=current_dst, send_sem=shift_sems.at[2], recv_sem=shift_sems.at[3],
         device_id={"tm": k + 1}, device_id_type=MESH,
     )
-    pl.when(has_after)(shift.start)
-
-    region_out, region_in = halo_copies(0, region_ref, region_buf)
-    gain_out, gain_in = halo_copies(1, gain_ref, gain_buf)
-    start(region_out)
-    start(gain_out)
+    pl.when(has_after)(current_shift.start)
 
     for d, planes in pieces:
         low = M - (d - 1) * block - planes
@@ -124,12 +143,10 @@
                 for number in range(4):
                     fields[number, pl.ds(place, planes)] = zero
 
-    region_buf[own] = region_ref[...]
-    gain_buf[own] = gain_ref[...]
-
     @pl.when(k == 0)
     def _():
         shift_dst[...] = jnp.zeros_like(shift_dst)
+        current_dst[...] = jnp.zeros_like(current_dst)
 
     for at, d in enumerate(distances):
         @pl.when(k < d)
@@ -140,7 +157,9 @@
     pl.when(has_before)(shift.wait_recv)
     w_out, w_in = halo_copies(2, shift_dst, fields.at[0])
     start(w_out)
-    fields[0, own] = shift_dst[pl.ds(0, block)]
+    fields[0, own] = shift_dst[...]
+    for load in loads[2:]:
+        load.wait()
 
     finish(region_in)
 
@@ -160,6 +179,7 @@
 
     lax.fori_loop(0, whole, coefficients, 0)
     finish(gain_in)
+    pl.when(has_before)(current_shift.wait_recv)
     finish(w_in)
 
     lane = lax.broadcasted_iota(jnp.int32, (ny, nz), 1)
@@ -191,7 +211,7 @@
                 for half, (source, target) in enumerate(((field, other), (other, field))):
                     current = None
                     if sourced:
-                        row = shift_dst[block, pl.ds(step + half, 1), :]
+                        row = current_dst[pl.ds(step + half, 1), :]
                         current = jnp.broadcast_to(row, (ny, nz))
                     fine_step(source, target, margin, current)
                 return 0
@@ -235,9 +255,9 @@
         return total
 
     propagate(fields.at[0], True)
-    before = jnp.where(k == 0, init_ref[...], fields[0, own])
+    before = jnp.where(k == 0, init_buf[...], fields[0, own])
     kept[0] = before
-    out_1 = exchange(3, before - w_ref[0])
+    out_1 = exchange(3, before - w_buf[...])
     propagate(fields.at[1], False)
 
     factor = factor_buf[own]
@@ -255,9 +275,10 @@
 
     scan(1, defect, factor)
     corrected = kept[0] + scan_dst[1, 0] + factor * two_back(1, factor)
-    out_ref[0] = jnp.where(k == 0, init_ref[...], corrected)
+    out_ref[0] = jnp.where(k == 0, init_buf[...], corrected)
 
     pl.when(has_after)(shift.wait_send)
+    pl.when(has_after)(current_shift.wait_send)
     for copies in (region_out, gain_out, w_out, out_1, out_2, out_3, pending):
         drain(copies)
 
@@ -270,16 +291,23 @@
     whole = block + 2 * M
     pieces, laps = 2 * len(halo_pieces(block)), len(scan_distances(times))
     vmem = pl.BlockSpec(memory_space=pltpu.VMEM)
-    smem = pl.BlockSpec(memory_space=pltpu.SMEM)
+    hbm = pl.BlockSpec(memory_space=pltpu.HBM)
     f32 = jnp.float32
     return pl.pallas_call(
         functools.partial(kernel, times, spaces, block),
         out_shape=(jax.ShapeDtypeStruct((1, block, ny, nz), f32),) * 2,
-        in_specs=[vmem] * 4 + [smem] * 4,
+        in_specs=[hbm] * 8,
         out_specs=(vmem, vmem),
         scratch_shapes=[
-            pltpu.VMEM((block + 1, ny, nz), f32),
-            pltpu.VMEM((block + 1, ny, nz), f32),
+            pltpu.VMEM((block, ny, nz), f32),
+            pltpu.VMEM((block, ny, nz), f32),
+            pltpu.SMEM(conductivity.shape, f32),
+            pltpu.SMEM(loss_table.shape, f32),
+            pltpu.SMEM(levels.shape, f32),
+            pltpu.SMEM(plan.shape, plan.dtype),
+            pltpu.VMEM((ny, nz), f32),
+            pltpu.VMEM((ny, nz), f32),
+            pltpu.VMEM((block, ny, nz), f32),
             pltpu.VMEM((whole, ny, nz), jnp.int32),
             pltpu.VMEM((whole, ny, nz), f32),
             pltpu.VMEM((4, whole, ny, nz), f32),
@@ -293,12 +321,13 @@
             pltpu.VMEM((1, block, ny, nz), f32),
             pltpu.SemaphoreType.DMA((6, pieces)),
             pltpu.SemaphoreType.DMA((6, pieces)),
-            pltpu.SemaphoreType.DMA((2,)),
+            pltpu.SemaphoreType.DMA((4,)),
             pltpu.SemaphoreType.DMA((2, laps)),
             pltpu.SemaphoreType.DMA((2, laps)),
+            pltpu.SemaphoreType.DMA((8,)),
         ],
         compiler_params=pltpu.CompilerParams(
-            collective_id=0, has_side_effects=True, vmem_limit_bytes=16 * 1024 * 1024
+            collective_id=0, has_side_effects=True, vmem_limit_bytes=64 * 1024 * 1024
         ),
     )(initial_guess, region, heat_gain, initial_state, conductivity, loss_table, levels, plan)
 

time: 47 us -> 40.5 us (0.86)
  local copies, waits for them, and re-layouts: 7.23 us -> 2.14 us
  Pallas kernels: 38.8 us -> 37.5 us
    unnamed x18 -> x4, local copies, waits for them, and re-layouts: 7.23 us -> 2.14 us
    pallas_call x1, Pallas kernels: 38.8 us -> 37.5 us  [on_device(): pl.pallas_call(functools.partial(kernel, times, spaces, block), out_shape...]
where the time goes in v2:
time: 40.5 us; the launch traced here: 40.3 us
  Pallas kernels  37.5 us (93%)
  local copies, waits for them, and re-layouts  2.14 us (5%)
  between operations  0.65 us (2%)
    pallas_call x1, Pallas kernels, on_device(): pl.pallas_call(functools.partial(kernel, times, spaces, block), out_shape...  37.5 us
    unnamed x4, local copies, waits for them, and re-layouts  2.14 us

profile of v2, /device:TPU:30, one launch (start us, length us, event | category | flops | bytes accessed | tf_op | source)
XLA Modules:
  0.0 40.3 jit_solution(10955249044079671156)
XLA Ops:
  0.6 37.5 %shard_map.95 = (f32[1,8,16,128]{3,2,1,0:T(8,128)}, f32[1,8,16,128]{3,2,1,0:T(8,128)}) custom-call(f32[1,8,16,128]{3,2,1,0:T(8,128)} %w_ref.1, s32[8,16,128]{2,1,0:T(8,128)} %region_ref.1, f32[8,16,128]{2,1,0:T(8,128)} %gain_ref.1, f32[8,16,128]{2,1,0:T(8,128)} %init_ref.1, f32[8]{0:T(128)} %conduct_hbm.1, f32[8]{0:T(128)} %loss_hbm.1, f32[8]{0:T(128)} %levels_hbm.1, ...), custom_call_target="tpu_custom_call" | custom-call | tf_op jit(solution)/shard_map/pallas_call | solution.py:296
  38.2 0.0 copy-start
  38.2 1.5 %copy.12 = f32[1,8,16,128]{3,2,1,0:T(8,128)} copy(f32[1,8,16,128]{3,2,1,0:T(8,128)} %get-tuple-element.4) | data formatting | bytes 131072
  39.7 0.0 copy-done
  39.7 0.6 %copy.13 = f32[1,8,16,128]{3,2,1,0:T(8,128)} copy(f32[1,8,16,128]{3,2,1,0:T(8,128)S(1)} %copy-done) | data formatting | bytes 131072
Async XLA Ops:
  38.2 1.5 %copy-start = (f32[1,8,16,128]{3,2,1,0:T(8,128)S(1)}, f32[1,8,16,128]{3,2,1,0:T(8,128)}, u32[]{:S(2)}) copy-start(f32[1,8,16,128]{3,2,1,0:T(8,128)} %get-tuple-element.5) | copy-start | bytes 196612

commit v3 on v2

--- a/solution.py
+++ b/solution.py
@@ -32,7 +32,7 @@
 def kernel(
     times, spaces, block,
     w_ref, region_ref, gain_ref, init_ref, conduct_hbm, loss_hbm, levels_hbm, plan_hbm,
-    out_ref, defect_ref,
+    both_ref,
     w_buf, init_buf, conduct_ref, loss_ref, levels_ref, plan_ref,
     current_src, current_dst, shift_dst, region_buf, gain_buf, fields, other, diag_buf, spread_buf, factor_buf,
     sends, scan_src, scan_dst, kept,
@@ -271,11 +271,11 @@
     out_3 = exchange(5, relaxed - factor * sends[1])
     propagate(fields.at[3], False)
     defect = fields[3, own]
-    defect_ref[0] = defect
+    both_ref[1] = defect
 
     scan(1, defect, factor)
     corrected = kept[0] + scan_dst[1, 0] + factor * two_back(1, factor)
-    out_ref[0] = jnp.where(k == 0, init_buf[...], corrected)
+    both_ref[0] = jnp.where(k == 0, init_buf[...], corrected)
 
     pl.when(has_after)(shift.wait_send)
     pl.when(has_after)(current_shift.wait_send)
@@ -293,11 +293,11 @@
     vmem = pl.BlockSpec(memory_space=pltpu.VMEM)
     hbm = pl.BlockSpec(memory_space=pltpu.HBM)
     f32 = jnp.float32
-    return pl.pallas_call(
+    both = pl.pallas_call(
         functools.partial(kernel, times, spaces, block),
-        out_shape=(jax.ShapeDtypeStruct((1, block, ny, nz), f32),) * 2,
+        out_shape=jax.ShapeDtypeStruct((2, block, ny, nz), f32),
         in_specs=[hbm] * 8,
-        out_specs=(vmem, vmem),
+        out_specs=vmem,
         scratch_shapes=[
             pltpu.VMEM((block, ny, nz), f32),
             pltpu.VMEM((block, ny, nz), f32),
@@ -330,6 +330,7 @@
             collective_id=0, has_side_effects=True, vmem_limit_bytes=64 * 1024 * 1024
         ),
     )(initial_guess, region, heat_gain, initial_state, conductivity, loss_table, levels, plan)
+    return both[:1], both[1:]
 
 
 def solution(mesh):

time: 40.5 us -> 39.9 us (0.985)
  local copies, waits for them, and re-layouts: 2.14 us -> 1.53 us
    unnamed x4 -> x0, local copies, waits for them, and re-layouts: 2.14 us -> none
    slice x0 -> x1, local copies, waits for them, and re-layouts: none -> 1.53 us  [on_device(): return (both[:1], both[1:])]
where the time goes in v3:
time: 39.9 us; the launch traced here: 39.7 us
  Pallas kernels  37.5 us (94%)
  local copies, waits for them, and re-layouts  1.53 us (4%)
  between operations  0.64 us (2%)
    pallas_call x1, Pallas kernels, on_device(): pl.pallas_call(functools.partial(kernel, times, spaces, block), out_shape...  37.5 us
    slice x1, local copies, waits for them, and re-layouts, on_device(): return (both[:1], both[1:])  1.53 us

profile of v3, /device:TPU:30, one launch (start us, length us, event | category | flops | bytes accessed | tf_op | source)
XLA Modules:
  0.0 39.7 jit_solution(7019001500030913401)
XLA Ops:
  0.6 37.5 %shard_map.95 = f32[2,8,16,128]{3,2,1,0:T(8,128)} custom-call(f32[1,8,16,128]{3,2,1,0:T(8,128)} %w_ref.1, s32[8,16,128]{2,1,0:T(8,128)} %region_ref.1, f32[8,16,128]{2,1,0:T(8,128)} %gain_ref.1, f32[8,16,128]{2,1,0:T(8,128)} %init_ref.1, f32[8]{0:T(128)} %conduct_hbm.1, f32[8]{0:T(128)} %loss_hbm.1, f32[8]{0:T(128)} %levels_hbm.1, s32[12]{0:T(128)} %plan_hbm.1), custom_call_target="tpu_custom_call" | custom-call | tf_op jit(solution)/shard_map/pallas_call | solution.py:296
  38.2 1.5 %fusion = (f32[1,8,16,128]{3,2,1,0:T(8,128)}, f32[1,8,16,128]{3,2,1,0:T(8,128)}) fusion(f32[2,8,16,128]{3,2,1,0:T(8,128)} %shard_map.95), kind=kLoop, calls=%fused_computation | loop fusion | bytes 262144 | tf_op jit(solution)/shard_map/slice | solution.py:333
